TPU v7x, 128 devices: a whole 4x4x4 slice. The times are simulated.
128 devices in a mesh: row: 8 (over y, x_hi), col: 16 (over z, x_lo, core).
Axes of the slice: x: 4 (x_hi: 2, x_lo: 2; x = x_hi * 2 + x_lo), y: 4, z: 4, core: 2. Of those that a mesh axis runs over, the one named last changes fastest.
Arguments:
- ham_tiles: float32 [8, 16, 320, 128, 128], P('row', 'col'), may hold values from -0.0625 to 0.0625
- tile_list: int32 [8, 16, 320, 2], P('row', 'col'), may hold values from 0 to 63, as said below
- tile_count: int32 [8, 16], P('row', 'col'), may hold values from 1 to 320, as said below
- basis_block: float32 [16, 65536], P(None, ('row', 'col')), may hold values from -6 to 6
- residual_block: float32 [16, 65536], P(None, ('row', 'col')), may hold values from -6 to 6
Outputs:
- h_basis: float32 [16, 65536], P(None, ('row', 'col'))
- h_residual: float32 [16, 65536], P(None, ('row', 'col'))
Inputs may be any that keep to these rules, and one draw needn't show every extreme that they name: `tile_list`: entry 0 is a block row within the grid row, below 64; entry 1 a block column within the grid column, below 32. Live slots name distinct blocks with global row block at most the global column block; slots past the count name arbitrary blocks in range. `tile_count`: each device's count lies between half and all of its share of 320 in proportion to its upper-triangle slots, never above its distinct upper blocks; devices with the most upper-triangle slots hold exactly 320.
All inputs are finite; a program needn't handle non-finite values.
Results may differ from a plain program's by a relative error of at most 0.0003.
Values sent between devices are 32-bit elements; how exact they have to be, the bound alone decides.
A program may use at most 128 MiB of HBM per device.

v0:
```python
import jax
import jax.numpy as jnp
from jax import lax
from jax.sharding import PartitionSpec as P


def tile_products(
    row_panel, col_panel, tile_data, local_row, local_col, row_weight, diag_weight, col_weight
):
    width = row_panel.shape[0]
    side = tile_data.shape[-1]
    row_blocks = row_panel.reshape(width, row_panel.shape[1] // side, side)
    col_blocks = col_panel.reshape(width, col_panel.shape[1] // side, side)
    picked_cols = jnp.take(col_blocks, local_col, axis=1)
    picked_rows = jnp.take(row_blocks, local_row, axis=1)
    fwd_terms = jnp.einsum("vtb,tab->vta", picked_cols, tile_data, precision=lax.Precision.HIGHEST)
    tr_terms = jnp.einsum("vta,tab->vtb", picked_rows, tile_data, precision=lax.Precision.HIGHEST)
    row_add = row_weight[None, :, None] * fwd_terms + diag_weight[None, :, None] * tr_terms
    col_add = col_weight[None, :, None] * tr_terms
    row_partial = jnp.zeros_like(row_blocks).at[:, local_row].add(row_add)
    col_partial = jnp.zeros_like(col_blocks).at[:, local_col].add(col_add)
    return (
        row_partial.reshape(width, row_panel.shape[1]),
        col_partial.reshape(width, col_panel.shape[1]),
    )


def apply_panel(stacked, tile_data, local_row, local_col, row_weight, diag_weight, col_weight):
    row_panel = lax.all_gather(stacked, "col", axis=1, tiled=True)
    col_panel = lax.all_gather(stacked, "row", axis=1, tiled=True)
    row_partial, col_partial = tile_products(
        row_panel, col_panel, tile_data, local_row, local_col, row_weight, diag_weight, col_weight
    )
    row_share = lax.psum_scatter(row_partial, "col", scatter_dimension=1, tiled=True)
    col_share = lax.psum_scatter(col_partial, "row", scatter_dimension=1, tiled=True)
    return row_share + col_share


def local(ham_tiles, tile_list, tile_count, basis_block, residual_block):
    side = ham_tiles.shape[-1]
    per_piece = basis_block.shape[1] // side
    row_blocks_count = per_piece * lax.axis_size("col")
    row_index = lax.axis_index("row")
    col_index = lax.axis_index("col")
    tile_data = ham_tiles[0, 0]
    listing = tile_list[0, 0]
    local_row = listing[:, 0]
    local_col = listing[:, 1]
    global_row = row_index * row_blocks_count + local_row
    global_col = (
        local_col // per_piece * row_blocks_count + col_index * per_piece + local_col % per_piece
    )
    live = (jnp.arange(tile_data.shape[0], dtype=jnp.int32) < tile_count[0, 0]).astype(jnp.float32)
    diag_flag = (global_row == global_col).astype(jnp.float32)
    row_weight = live * (1.0 - 0.5 * diag_flag)
    diag_weight = live * 0.5 * diag_flag
    col_weight = live * (1.0 - diag_flag)
    outputs = []
    for block in (basis_block, residual_block):
        outputs.append(
            apply_panel(block, tile_data, local_row, local_col, row_weight, diag_weight, col_weight)
        )
    h_basis = outputs[0]
    h_residual = outputs[1]
    return (h_basis, h_residual)


def solution(mesh):
    placed = (
        P("row", "col", None, None, None),
        P("row", "col", None, None),
        P("row", "col"),
        P(None, ("row", "col")),
        P(None, ("row", "col")),
    )
    return jax.shard_map(
        local,
        mesh=mesh,
        in_specs=placed,
        out_specs=(P(None, ("row", "col")), P(None, ("row", "col"))),
        check_vma=False,
    )
```

profile of v0, /device:TPU:6, one launch (start us, length us, event | category | flops | bytes accessed | tf_op | source)
XLA Modules:
  0.0 427.1 jit_solution(16979105326237246773)
XLA Ops:
  7.2 0.8 fusion.39
  8.0 20.1 %all_gather.13 = f32[16,8192]{1,0:T(8,128)S(1)} all-gather(f32[16,512]{1,0:T(8,128)} %param.12), channel_id=1, replica_groups=mesh['row'=8,'col'=16] {'col'}, dimensions={1}, use_global_device_ids=true | all-gather | bytes 557056 | tf_op jit(solution)/shard_map/all_gather | solution.py:29
  28.8 22.0 %all_gather.15 = f32[16,8192]{1,0:T(8,128)S(1)} all-gather(f32[16,512]{1,0:T(8,128)} %param.13), channel_id=1, replica_groups=mesh['row'=8,'col'=16] {'col'}, dimensions={1}, use_global_device_ids=true | all-gather | bytes 557056 | tf_op jit(solution)/shard_map/all_gather | solution.py:29
  50.9 2.6 gather_fusion.1
  53.6 2.7 gather_fusion.3
  56.2 21.2 %fusion.4 = f32[320,16,128]{2,1,0:T(8,128)S(1)} fusion(f32[1,1,320,128,128]{4,3,2,1,0:T(8,128)} %param.9, f32[320,16,128]{2,1,0:T(8,128)} %gather_fusion.1, pred[320]{0:T(512)(128)(4,1)S(1)} %compare_and_fusion), kind=kOutput, calls=%fused_computation.12 | convolution fusion | flops 1007288320 | bytes 26214720 | tf_op jit(solution)/shard_map/vta,tab->vtb/dot_general | solution.py:17
  77.5 22.2 %broadcast_multiply_fusion = (f32[320,16,128]{2,1,0:T(8,128)}, f32[320,16,128]{2,1,0:T(8,128)}, f32[320,16,128]{2,1,0:T(8,128)}) fusion(f32[320]{0:T(512)S(1)} %get-tuple-element.8, f32[320,16,128]{2,1,0:T(8,128)S(1)} %fusion.4, f32[1,1,320,128,128]{4,3,2,1,0:T(8,128)} %param.9, f32[320,16,128]{2,1,0:T(8,128)S(1)} %copy-done.2, ...), kind=kOutput, calls=%fused_computation.30 | convolution fusion | flops 1008599040 | bytes 34080320 | tf_op jit(solution)/shard_map/vta,tab->vtb/dot_general | solution.py:17
  99.7 25.7 %scatter_fusion.1 = f32[16,32,128]{2,0,1:T(8,128)S(1)} fusion(f32[16,32,128]{2,0,1:T(8,128)S(1)} %broadcast.251.clone, s32[320]{0:T(512)S(1)} %get-tuple-element.4, f32[320,16,128]{2,1,0:T(8,128)} %get-tuple-element.11), kind=kCustom, calls=%fused_computation.5 | custom fusion | flops 655360 | bytes 7865600 | tf_op jit(solution)/shard_map/scatter-add | solution.py:21
  125.4 0.7 copy_bitcast_fusion.5
  126.2 35.3 %all_gather.12 = f32[16,4096]{1,0:T(8,128)S(1)} all-gather(f32[16,512]{1,0:T(8,128)S(1)} %copy-done.3), channel_id=1, replica_groups=mesh['row'=8,'col'=16] {'row'}, dimensions={1}, use_global_device_ids=true | all-gather | bytes 294912 | tf_op jit(solution)/shard_map/all_gather | solution.py:30
  161.6 2.6 gather_fusion
  164.3 36.7 %multiply_add_fusion.1 = f32[320,16,128]{2,1,0:T(8,128)} fusion(f32[320,16,128]{2,1,0:T(8,128)S(1)} %fusion.4, f32[1,1,320,128,128]{4,3,2,1,0:T(8,128)} %param.9, f32[320,16,128]{2,1,0:T(8,128)} %gather_fusion, f32[320]{0:T(512)S(1)} %get-tuple-element.13, f32[320]{0:T(512)S(1)} %get-tuple-element.12, pred[320]{0:T(512)(128)(4,1)S(1)} %compare_and_fusion.1), kind=kOutput, calls=%fused_computation.25 | convolution fusion | flops 1009254400 | bytes 28838720 | tf_op jit(solution)/shard_map/vtb,tab->vta/dot_general | solution.py:16
  201.0 25.8 %scatter_fusion = f32[16,64,128]{2,0,1:T(8,128)S(1)} fusion(f32[16,64,128]{2,0,1:T(8,128)S(1)} %broadcast.243.clone, s32[320]{0:T(512)S(1)} %get-tuple-element.5, f32[320,16,128]{2,1,0:T(8,128)} %multiply_add_fusion.1), kind=kCustom, calls=%fused_computation.4 | custom fusion | flops 655360 | bytes 7865600 | tf_op jit(solution)/shard_map/scatter-add | solution.py:20
  226.8 0.8 copy_bitcast_fusion.1
  227.7 12.4 %scatter_fusion.3 = f32[16,32,128]{2,0,1:T(8,128)S(1)} fusion(f32[16,32,128]{2,0,1:T(8,128)S(1)} %broadcast.251.clone.1, s32[320]{0:T(512)S(1)} %get-tuple-element.4, f32[320,16,128]{2,1,0:T(8,128)S(1)} %copy-done.1), kind=kCustom, calls=%fused_computation.7 | custom fusion | flops 655360 | bytes 7865600 | tf_op jit(solution)/shard_map/scatter-add | solution.py:21
  240.9 36.0 %all_gather.14 = f32[16,4096]{1,0:T(8,128)S(1)} all-gather(f32[16,512]{1,0:T(8,128)S(1)} %copy-done.4), channel_id=1, replica_groups=mesh['row'=8,'col'=16] {'row'}, dimensions={1}, use_global_device_ids=true | all-gather | bytes 294912 | tf_op jit(solution)/shard_map/all_gather | solution.py:30
  276.9 2.7 gather_fusion.2
  279.6 36.6 %multiply_add_fusion = f32[320,16,128]{2,1,0:T(8,128)} fusion(f32[320,16,128]{2,1,0:T(8,128)S(1)} %copy-done, f32[1,1,320,128,128]{4,3,2,1,0:T(8,128)} %param.9, f32[320,16,128]{2,1,0:T(8,128)} %gather_fusion.2, f32[320]{0:T(512)S(1)} %get-tuple-element.13, f32[320]{0:T(512)S(1)} %get-tuple-element.12, pred[320]{0:T(512)(128)(4,1)S(1)} %compare_and_fusion.1), kind=kOutput, calls=%fused_computation.24 | convolution fusion | flops 1009254400 | bytes 28838720 | tf_op jit(solution)/shard_map/vtb,tab->vta/dot_general | solution.py:16
  316.2 25.6 %scatter_fusion.2 = f32[16,64,128]{2,0,1:T(8,128)S(1)} fusion(f32[16,64,128]{2,0,1:T(8,128)S(1)} %broadcast.243.clone.1, s32[320]{0:T(512)S(1)} %get-tuple-element.5, f32[320,16,128]{2,1,0:T(8,128)} %multiply_add_fusion), kind=kCustom, calls=%fused_computation.6 | custom fusion | flops 655360 | bytes 7865600 | tf_op jit(solution)/shard_map/scatter-add | solution.py:20
  341.8 0.8 copy_bitcast_fusion
  342.8 1.4 add.138
  344.1 15.9 %reduce-scatter.11.cloned.1.call-done = f32[16,512]{1,0:T(8,128)} async-done(((f32[16,4096]{1,0:T(8,128)}), f32[16,512]{1,0:T(8,128)}) %reduce-scatter.11.cloned.1.call-update) | async-done | bytes 32784 | tf_op jit(solution)/shard_map/reduce_scatter | solution.py:35
  360.1 59.0 %reduce-scatter.9.cloned.1.call-done = f32[16,512]{1,0:T(8,128)} async-done(((f32[16,8192]{1,0:T(8,128)}), f32[16,512]{1,0:T(8,128)}) %reduce-scatter.9.cloned.1.call-update) | async-done | bytes 32784 | tf_op jit(solution)/shard_map/reduce_scatter | solution.py:34
  419.1 1.4 add.141
  (37 shorter events, 1.3 us)
Async XLA Ops:
  7.2 335.6 %reduce-scatter.7.cloned.1.call-start = ((), (), s32[]{:S(2)}) async-start(), calls=%async_computation.5 | async-start | bytes 294912 | tf_op jit(solution)/shard_map/reduce_scatter | solution.py:35
  56.2 21.3 %copy-start.2 = (f32[320,16,128]{2,1,0:T(8,128)S(1)}, f32[320,16,128]{2,1,0:T(8,128)}, u32[]{:S(2)}) copy-start(f32[320,16,128]{2,1,0:T(8,128)} %gather_fusion.3) | copy-start | bytes 7864324
  99.7 26.5 %copy-start.3 = (f32[16,512]{1,0:T(8,128)S(1)}, f32[16,512]{1,0:T(8,128)}, u32[]{:S(2)}) copy-start(f32[16,512]{1,0:T(8,128)} %param.12) | copy-start | bytes 98308
  126.2 216.6 %reduce-scatter.5.cloned.1.call-start = ((), (), s32[]{:S(2)}) async-start(), calls=%async_computation.4 | async-start | bytes 557056 | tf_op jit(solution)/shard_map/reduce_scatter | solution.py:34
  201.0 26.8 %copy-start.1 = (f32[320,16,128]{2,1,0:T(8,128)S(1)}, f32[320,16,128]{2,1,0:T(8,128)}, u32[]{:S(2)}) copy-start(f32[320,16,128]{2,1,0:T(8,128)} %get-tuple-element.10) | copy-start | bytes 7864324
  227.6 132.5 %reduce-scatter.11.cloned.1.call-start = ((), (), s32[]{:S(2)}) async-start(), calls=%async_computation.7 | async-start | bytes 294912 | tf_op jit(solution)/shard_map/reduce_scatter | solution.py:35
  227.7 13.2 %copy-start.4 = (f32[16,512]{1,0:T(8,128)S(1)}, f32[16,512]{1,0:T(8,128)}, u32[]{:S(2)}) copy-start(f32[16,512]{1,0:T(8,128)} %param.13) | copy-start | bytes 98308
  240.9 178.3 %reduce-scatter.9.cloned.1.call-start = ((), (), s32[]{:S(2)}) async-start(), calls=%async_computation.6 | async-start | bytes 557056 | tf_op jit(solution)/shard_map/reduce_scatter | solution.py:34
  276.9 2.7 copy-start
Sparse Core Ops, SparseCore 0:
  126.3 68.4 reduce-scatter.6
  227.8 56.6 reduce-scatter.4
  288.4 71.6 reduce-scatter.10
  362.4 56.6 reduce-scatter.8
where the time goes:
time: 432 us; the launch traced here: 427 us
  matrix products  117 us (27%)
  blocking collectives  113 us (26%)
  other arithmetic  93.1 us (22%)
  waiting for transfers between devices  75.1 us (17%)
  between operations  14.6 us (3%)
  local copies, waits for them, and re-layouts  13.9 us (3%)
    dot_general x2, matrix products, tile_products(): jnp.einsum('vtb,tab->vta', picked_cols, tile_data, precision=lax.Precisio...  73.3 us
    all_gather x2, blocking collectives, apply_panel(): col_panel = lax.all_gather(stacked, 'row', axis=1, tiled=True)  71.3 us
    reduce_scatter x2, waiting for transfers between devices, apply_panel(): lax.psum_scatter(row_partial, 'col', scatter_dimension=1, tiled=True)  59.1 us
    scatter-add x2, other arithmetic, tile_products(): row_partial = jnp.zeros_like(row_blocks).at[:, local_row].add(row_add)  51.4 us
    dot_general x2, matrix products, tile_products(): jnp.einsum('vta,tab->vtb', picked_rows, tile_data, precision=lax.Precisio...  43.4 us
    all_gather x2, blocking collectives, apply_panel(): row_panel = lax.all_gather(stacked, 'col', axis=1, tiled=True)  42.2 us
    scatter-add x2, other arithmetic, tile_products(): col_partial = jnp.zeros_like(col_blocks).at[:, local_col].add(col_add)  38 us
    reduce_scatter x2, waiting for transfers between devices, apply_panel(): lax.psum_scatter(col_partial, 'row', scatter_dimension=1, tiled=True)  16 us
  transfers between devices with their start and end apart: 4, of which 2 were waited for; matrix products, arithmetic and copies ran while one was open for 34% of the time, Pallas kernels for 0%

commit v1 on v0

v1 whole, which is shorter than its diff:
```python
import functools

import jax
import jax.numpy as jnp
from jax import lax
from jax.experimental import pallas as pl
from jax.experimental.pallas import tpu as pltpu
from jax.sharding import PartitionSpec as P

MESH = pl.DeviceIdType.MESH
TILE = 128
BP = 4
NT = (((1,), (1,)), ((), ()))
NN = (((1,), (0,)), ((), ()))
BF = jnp.bfloat16
F32 = jnp.float32
I32 = jnp.int32


def split2(value):
    hi = value.astype(BF)
    lo = (value - hi.astype(F32)).astype(BF)
    return hi, lo


def put_operand(dst, index, block):
    rows = block.shape[0]
    hi, lo = split2(block)
    dst[index, :rows, :TILE] = hi
    dst[index, :rows, TILE:] = hi
    dst[index, rows:, :TILE] = lo
    dst[index, rows:, TILE:] = jnp.zeros_like(lo)


def row_of(column, spot):
    return jnp.sum(jnp.where(spot, column, 0), axis=0, keepdims=True)


def sorted_lists(key, other, weight2, iota0, iota1, slots):
    tagged = key * 512 + iota0[:, :1]
    tagged_row = row_of(tagged, iota0 == iota1)
    real = iota1 < slots
    rank = jnp.sum(jnp.where((tagged_row < tagged) & real, 1, 0), axis=1, keepdims=True)
    earlier = (tagged_row < tagged) & real & (tagged_row >= key * 512)
    repeats = jnp.minimum(
        jnp.sum(jnp.where(earlier, 1, 0), axis=1, keepdims=True), 1
    )
    place = rank == iota1
    return (
        row_of(iota0[:, :1], place),
        row_of(other, place),
        row_of(repeats, place),
        row_of(weight2, place),
    )


def segment_ends(key, lanes):
    last = jnp.sum(jnp.where(key <= lanes, 1, 0), axis=0, keepdims=True) - 1
    some = jnp.minimum(jnp.sum(jnp.where(key == lanes, 1, 0), axis=0, keepdims=True), 1)
    return jnp.maximum(last, 0), some


def kernel(
    n_row,
    n_col,
    unroll,
    chunks,
    list_ref,
    count_ref,
    basis_ref,
    residual_ref,
    tiles_ref,
    out_basis,
    out_residual,
    raw,
    halves,
    running,
    row_raw,
    col_raw,
    row_x,
    col_x,
    row_part,
    from_twin,
    from_row,
    col_part,
    from_col,
    lists_v,
    lists_s,
    marks_v,
    marks_s,
    tile_sem,
    list_sem,
    far_send,
    far_recv,
    twin_send,
    twin_recv,
    up_send,
    up_recv,
    fold_sem,
    back_send,
    back_recv,
    down_send,
    down_recv,
):
    slots = halves.shape[0]
    width = row_raw.shape[2]
    half = width // 2
    chips = n_col // 2
    per = slots // chunks
    r = lax.axis_index("row")
    c = lax.axis_index("col")
    core = c % 2
    chip = c // 2
    twin = chip * 2 + 1 - core
    zs, z, xl = chips // 2, chip // 2, chip % 2

    def chip_at(d):
        return ((z + d // 2) % zs) * 2 + (xl + d % 2) % 2

    def tile_copy(k):
        part = pl.ds(k * per, per)
        return pltpu.make_async_copy(
            tiles_ref.at[0, 0, part], raw.at[part], tile_sem.at[k]
        )

    def remote(src, dst, send, recv, row, col):
        return pltpu.make_async_remote_copy(
            src_ref=src,
            dst_ref=dst,
            send_sem=send,
            recv_sem=recv,
            device_id=(row, col),
            device_id_type=MESH,
        )

    for k in range(chunks):
        tile_copy(k).start()

    for b in range(BP):
        columns = slice(b * TILE, (b + 1) * TILE)
        row_raw[c, b, :half] = basis_ref[:, columns]
        row_raw[c, b, half:] = residual_ref[:, columns]
        col_raw[r, b, :half] = basis_ref[:, columns]
        col_raw[r, b, half:] = residual_ref[:, columns]
    for g in range(n_row):

        @pl.when(g < r)
        def _():
            col_raw[g] = jnp.zeros(col_raw.shape[1:], F32)

    barrier = pltpu.get_barrier_semaphore()
    for d in range(1, n_row):
        pl.semaphore_signal(
            barrier, inc=1, device_id=((r + d) % n_row, c), device_id_type=MESH
        )
    pl.semaphore_signal(barrier, inc=1, device_id=(r, twin), device_id_type=MESH)
    for d in range(1, chips):
        pl.semaphore_signal(
            barrier, inc=1, device_id=(r, chip_at(d) * 2 + core), device_id_type=MESH
        )
    pl.semaphore_wait(barrier, n_row - 1 + 1 + chips - 1)

    def up_copy(d):
        return remote(
            col_raw.at[r], col_raw.at[r], up_send.at[d], up_recv.at[r], (r + n_row - d) % n_row, c
        )

    def up_arrival(g):
        return remote(col_raw.at[g], col_raw.at[g], up_send.at[0], up_recv.at[g], r, twin)

    def far_copy(d):
        return remote(
            row_raw.at[c],
            row_raw.at[c],
            far_send.at[d],
            far_recv.at[chip],
            r,
            chip_at(d) * 2 + core,
        )

    def far_arrival(q):
        piece = row_raw.at[q * 2 + core]
        return remote(piece, piece, far_send.at[0], far_recv.at[q], r, twin)

    def twin_copy(q):
        piece = row_raw.at[q * 2 + core]
        return remote(piece, piece, twin_send.at[q], twin_recv.at[q], r, twin)

    def twin_arrival(q):
        piece = row_raw.at[q * 2 + 1 - core]
        return remote(piece, piece, twin_send.at[0], twin_recv.at[q], r, twin)

    for d in range(n_row - 1, 0, -1):

        @pl.when(d <= r)
        def _():
            up_copy(d).start()

    twin_copy(chip).start()
    for d in range(1, chips):
        far_copy(d).start()

    padded = lists_v.shape[1]
    iota0 = lax.broadcasted_iota(I32, (slots, padded), 0)
    iota1 = lax.broadcasted_iota(I32, (slots, padded), 1)
    listing = list_ref[0, 0]
    local_row = listing[:, 0:1]
    local_col = listing[:, 1:2]
    slot = iota0[:, :1]
    diagonal = (r * (n_col * BP) + local_row) == (
        (local_col // BP) * (n_col * BP) + c * BP + local_col % BP
    )
    weight2 = jnp.where(slot < count_ref[0, 0], jnp.where(diagonal, 1, 2), 0)
    by_row = sorted_lists(local_row, local_col, weight2, iota0, iota1, slots)
    by_col = sorted_lists(local_col, local_row, weight2, iota0, iota1, slots)
    lanes = lax.broadcasted_iota(I32, (slots, TILE), 1)
    row_end, row_some = segment_ends(local_row, lanes)
    col_end, col_some = segment_ends(local_col, lanes)
    for k, (order, other, again, weight) in enumerate((by_row, by_col)):
        lists_v[2 * k : 2 * k + 1] = order
        lists_v[2 * k + 1 : 2 * k + 2] = other
        marks_v[2 * k : 2 * k + 1] = again.astype(F32)
        marks_v[2 * k + 1 : 2 * k + 2] = weight.astype(F32) * 0.5
    lists_v[4:5, :TILE] = row_end
    lists_v[5:6, :TILE] = col_end
    marks_v[4:5, :TILE] = row_some.astype(F32)
    marks_v[5:6, :TILE] = col_some.astype(F32)
    lists_copy = pltpu.make_async_copy(lists_v, lists_s, list_sem.at[0])
    marks_copy = pltpu.make_async_copy(marks_v, marks_s, list_sem.at[1])
    lists_copy.start()
    marks_copy.start()

    group = 8

    @pl.loop(0, chunks)
    def _(k):
        tile_copy(k).wait()

        @pl.loop(0, per // group)
        def _(s):
            for u in range(group):
                t = k * per + s * group + u
                hi, lo = split2(raw[t])
                halves[t, :TILE] = hi
                halves[t, TILE:] = lo

    lists_copy.wait()
    marks_copy.wait()

    for g in range(1, n_row):

        @pl.when(g > r)
        def _():
            up_arrival(g).wait_recv()

    @pl.loop(0, n_row)
    def _(g):
        for b in range(BP):
            put_operand(col_x, g * BP + b, col_raw[g, b])

    def products(which, operand, forward, between):
        order_at, other_at = 2 * which, 2 * which + 1

        def body(s, total):
            between(s)
            for u in range(unroll):
                k = s * unroll + u
                t = lists_s[order_at, k]
                o = lists_s[other_at, k]
                tile = halves[t]
                if forward:
                    tile = jnp.concatenate([tile[:TILE], tile[TILE:]], axis=1)
                term = lax.dot_general(
                    operand[o], tile, NT if forward else NN, preferred_element_type=F32
                )
                term = term[:width] + term[width:]
                total = total * marks_s[2 * which, k] + term * marks_s[2 * which + 1, k]
                running[k] = total
            return total

        lax.fori_loop(0, slots // unroll, body, jnp.zeros((width, TILE), F32))

    def hand_over(s):
        @pl.when((s >= 1) & (s < chips))
        def _():
            q = chip_at(s)
            far_arrival(q).wait_recv()
            twin_copy(q).start()

    assert slots // unroll >= chips
    products(0, col_x, True, hand_over)

    @pl.loop(0, n_col)
    def _(p):
        for b in range(BP):
            k = lists_s[4, p * BP + b]
            row_part[p % 2, p // 2, b] = running[k] * marks_s[4, p * BP + b]

    fold = remote(
        row_part.at[1 - core], from_twin, fold_sem.at[0], fold_sem.at[1], r, twin
    )
    fold.start()

    for q in range(chips):
        twin_arrival(q).wait_recv()

    @pl.loop(0, n_col)
    def _(p):
        for b in range(BP):
            put_operand(row_x, p * BP + b, row_raw[p, b])

    def back_copy(d):
        q = chip_at(d)
        return remote(
            row_part.at[core, q],
            from_row.at[chip],
            back_send.at[d],
            back_recv.at[chip],
            r,
            q * 2 + core,
        )

    def back_arrival(d):
        q = chip_at(d)
        return remote(
            from_row.at[q], from_row.at[q], back_send.at[0], back_recv.at[q], r, twin
        )

    def fold_in(s):
        @pl.when(s == 2)
        def _():
            fold.wait_recv()
            for d in range(chips):
                q = chip_at(d)
                row_part[core, q] = row_part[core, q] + from_twin[q]
                if d > 0:
                    back_copy(d).start()

    products(1, row_x, False, fold_in)

    @pl.loop(0, n_row)
    def _(g):
        for b in range(BP):
            k = lists_s[5, g * BP + b]
            col_part[g, b] = running[k] * marks_s[5, g * BP + b]

    def down_copy(d):
        g = (r + d) % n_row
        return remote(
            col_part.at[g], from_col.at[r], down_send.at[d], down_recv.at[r], g, c
        )

    def down_arrival(g):
        return remote(
            from_col.at[g], from_col.at[g], down_send.at[0], down_recv.at[g], r, twin
        )

    for d in range(n_row - 1, 0, -1):

        @pl.when(r + d < n_row)
        def _():
            down_copy(d).start()

    row_part[core, chip] = row_part[core, chip] + col_part[r]
    for d in range(1, chips):
        back_arrival(d).wait_recv()
        row_part[core, chip] = row_part[core, chip] + from_row[chip_at(d)]
    for g in range(n_row - 1):

        @pl.when(g < r)
        def _():
            down_arrival(g).wait_recv()
            row_part[core, chip] = row_part[core, chip] + from_col[g]

    for b in range(BP):
        columns = slice(b * TILE, (b + 1) * TILE)
        out_basis[:, columns] = row_part[core, chip, b, :half]
        out_residual[:, columns] = row_part[core, chip, b, half:]

    for d in range(1, n_row):

        @pl.when(d <= r)
        def _():
            up_copy(d).wait_send()

        @pl.when(r + d < n_row)
        def _():
            down_copy(d).wait_send()

    for d in range(1, chips):
        far_copy(d).wait_send()
        back_copy(d).wait_send()
    for q in range(chips):
        twin_copy(q).wait_send()
    fold.wait_send()


def solution(mesh):
    n_row, n_col = mesh.shape["row"], mesh.shape["col"]
    chips = n_col // 2

    def local(ham_tiles, tile_list, tile_count, basis_block, residual_block):
        slots = ham_tiles.shape[2]
        width = 2 * basis_block.shape[0]
        padded = -(-slots // TILE) * TILE
        unroll = 20 if slots % 20 == 0 else 4
        chunks = 8
        vmem = pl.BlockSpec(memory_space=pltpu.VMEM)
        dma = pltpu.SemaphoreType.DMA
        piece = (BP, width, TILE)
        shape = jax.ShapeDtypeStruct(basis_block.shape, F32)
        return pl.pallas_call(
            functools.partial(kernel, n_row, n_col, unroll, chunks),
            out_shape=(shape, shape),
            in_specs=[
                vmem,
                pl.BlockSpec(memory_space=pltpu.SMEM),
                vmem,
                vmem,
                pl.BlockSpec(memory_space=pl.ANY),
            ],
            out_specs=(vmem, vmem),
            scratch_shapes=[
                pltpu.VMEM((slots, TILE, TILE), F32),
                pltpu.VMEM((slots, 2 * TILE, TILE), BF),
                pltpu.VMEM((slots, width, TILE), F32),
                pltpu.VMEM((n_col,) + piece, F32),
                pltpu.VMEM((n_row,) + piece, F32),
                pltpu.VMEM((n_col * BP, 2 * width, 2 * TILE), BF),
                pltpu.VMEM((n_row * BP, 2 * width, 2 * TILE), BF),
                pltpu.VMEM((2, chips) + piece, F32),
                pltpu.VMEM((chips,) + piece, F32),
                pltpu.VMEM((chips,) + piece, F32),
                pltpu.VMEM((n_row,) + piece, F32),
                pltpu.VMEM((n_row,) + piece, F32),
                pltpu.VMEM((8, padded), I32),
                pltpu.SMEM((8, padded), I32),
                pltpu.VMEM((8, padded), F32),
                pltpu.SMEM((8, padded), F32),
                dma((chunks,)),
                dma((2,)),
                dma((chips,)),
                dma((chips,)),
                dma((chips,)),
                dma((chips,)),
                dma((n_row,)),
                dma((n_row,)),
                dma((2,)),
                dma((chips,)),
                dma((chips,)),
                dma((n_row,)),
                dma((n_row,)),
            ],
            compiler_params=pltpu.CompilerParams(
                collective_id=0,
                has_side_effects=True,
                vmem_limit_bytes=60 * 2**20,
            ),
        )(tile_list, tile_count, basis_block, residual_block, ham_tiles)

    return jax.shard_map(
        local,
        mesh=mesh,
        in_specs=(
            P("row", "col", None, None, None),
            P("row", "col", None, None),
            P("row", "col"),
            P(None, ("row", "col")),
            P(None, ("row", "col")),
        ),
        out_specs=(P(None, ("row", "col")), P(None, ("row", "col"))),
        check_vma=False,
    )
```

time: 432 us -> 48 us (0.11)
  the two profiles are of different devices: /device:TPU:6 before, /device:TPU:9 now
where the time goes in v1:
time: 48 us; the launch traced here: 47.7 us
  Pallas kernels  42.1 us (88%)
  local copies, waits for them, and re-layouts  4.24 us (9%)
  between operations  1.29 us (3%)
    pallas_call x1, Pallas kernels, local(): pl.pallas_call(functools.partial(kernel, n_row, n_col, unroll, chunks), o...  42.1 us
    unnamed x3, local copies, waits for them, and re-layouts  4.24 us

profile of v1, /device:TPU:9, one launch (start us, length us, event | category | flops | bytes accessed | tf_op | source)
XLA Modules:
  0.0 47.7 jit_solution(5797884822360000621)
XLA Ops:
  1.3 1.5 %copy.7.list_ref = s32[1,1,320,2]{3,2,1,0:T(8,128)} copy(s32[1,1,320,2]{2,3,1,0:T(2,128)} %param.6) | data formatting | bytes 5120 | tf_op args[1]
  2.8 42.1 %shard_map.68 = (f32[16,512]{1,0:T(8,128)}, f32[16,512]{1,0:T(8,128)}) custom-call(s32[1,1,320,2]{3,2,1,0:T(8,128)} %copy.7.list_ref, s32[1,1]{1,0:T(1,128)S(6)} %copy.10.count_ref, f32[16,512]{1,0:T(8,128)} %basis_ref.1, f32[16,512]{1,0:T(8,128)} %residual_ref.1, f32[1,1,320,128,128]{4,3,2,1,0:T(8,128)} %tiles_ref.1), custom_call_target="tpu_custom_call" | custom-call | tf_op jit(solution)/shard_map/pallas_call | solution.py:412
  44.9 1.4 %copy.11 = f32[16,512]{1,0:T(8,128)} copy(f32[16,512]{1,0:T(8,128)} %get-tuple-element.4) | data formatting | bytes 65536
  46.3 1.4 %copy.12 = f32[16,512]{1,0:T(8,128)} copy(f32[16,512]{1,0:T(8,128)} %get-tuple-element.5) | data formatting | bytes 65536

commit v2 on v1

--- a/solution.py
+++ b/solution.py
@@ -36,12 +36,16 @@
     return jnp.sum(jnp.where(spot, column, 0), axis=0, keepdims=True)
 
 
+def column_of(row, spot):
+    return jnp.sum(jnp.where(spot, row, 0), axis=1, keepdims=True)
+
+
 def sorted_lists(key, other, weight2, iota0, iota1, slots):
     tagged = key * 512 + iota0[:, :1]
     tagged_row = row_of(tagged, iota0 == iota1)
-    real = iota1 < slots
-    rank = jnp.sum(jnp.where((tagged_row < tagged) & real, 1, 0), axis=1, keepdims=True)
-    earlier = (tagged_row < tagged) & real & (tagged_row >= key * 512)
+    before = (tagged_row < tagged) & (iota1 < slots)
+    rank = jnp.sum(jnp.where(before, 1, 0), axis=1, keepdims=True)
+    earlier = before & (tagged_row >= key * 512)
     repeats = jnp.minimum(
         jnp.sum(jnp.where(earlier, 1, 0), axis=1, keepdims=True), 1
     )
@@ -70,8 +74,7 @@
     basis_ref,
     residual_ref,
     tiles_ref,
-    out_basis,
-    out_residual,
+    out,
     raw,
     halves,
     running,
@@ -107,15 +110,18 @@
     half = width // 2
     chips = n_col // 2
     per = slots // chunks
+    blocks = n_col * BP
     r = lax.axis_index("row")
     c = lax.axis_index("col")
     core = c % 2
     chip = c // 2
     twin = chip * 2 + 1 - core
-    zs, z, xl = chips // 2, chip // 2, chip % 2
-
-    def chip_at(d):
-        return ((z + d // 2) % zs) * 2 + (xl + d % 2) % 2
+
+    upper = (n_row - 1 - r) * (BP * blocks) + BP * BP * c + BP * (BP + 1) // 2
+    most = (n_row - 1) * (BP * blocks) + BP * BP * (n_col - 1) + BP * (BP + 1) // 2
+    bound = jnp.minimum(slots * upper // most + 1, slots)
+    steps = (bound + unroll - 1) // unroll
+    parts = (bound + per - 1) // per
 
     def tile_copy(k):
         part = pl.ds(k * per, per)
@@ -133,7 +139,8 @@
             device_id_type=MESH,
         )
 
-    for k in range(chunks):
+    @pl.loop(0, parts)
+    def _(k):
         tile_copy(k).start()
 
     for b in range(BP):
@@ -149,33 +156,34 @@
             col_raw[g] = jnp.zeros(col_raw.shape[1:], F32)
 
     barrier = pltpu.get_barrier_semaphore()
-    for d in range(1, n_row):
+
+    @pl.loop(r + 1, n_row)
+    def _(g):
+        pl.semaphore_signal(barrier, inc=1, device_id=(g, c), device_id_type=MESH)
+
+    @pl.loop(chip + 1, chips)
+    def _(q):
         pl.semaphore_signal(
-            barrier, inc=1, device_id=((r + d) % n_row, c), device_id_type=MESH
-        )
-    pl.semaphore_signal(barrier, inc=1, device_id=(r, twin), device_id_type=MESH)
-    for d in range(1, chips):
-        pl.semaphore_signal(
-            barrier, inc=1, device_id=(r, chip_at(d) * 2 + core), device_id_type=MESH
-        )
-    pl.semaphore_wait(barrier, n_row - 1 + 1 + chips - 1)
-
-    def up_copy(d):
-        return remote(
-            col_raw.at[r], col_raw.at[r], up_send.at[d], up_recv.at[r], (r + n_row - d) % n_row, c
-        )
+            barrier, inc=1, device_id=(r, q * 2 + core), device_id_type=MESH
+        )
+
+    @pl.when(core == 0)
+    def _():
+        pl.semaphore_signal(barrier, inc=1, device_id=(r, twin), device_id_type=MESH)
+
+    @pl.when(r + chip + core > 0)
+    def _():
+        pl.semaphore_wait(barrier, r + chip + core)
+
+    def up_copy(g):
+        return remote(col_raw.at[r], col_raw.at[r], up_send.at[g], up_recv.at[r], g, c)
 
     def up_arrival(g):
         return remote(col_raw.at[g], col_raw.at[g], up_send.at[0], up_recv.at[g], r, twin)
 
-    def far_copy(d):
+    def far_copy(q):
         return remote(
-            row_raw.at[c],
-            row_raw.at[c],
-            far_send.at[d],
-            far_recv.at[chip],
-            r,
-            chip_at(d) * 2 + core,
+            row_raw.at[c], row_raw.at[c], far_send.at[q], far_recv.at[chip], r, q * 2 + core
         )
 
     def far_arrival(q):
@@ -190,32 +198,38 @@
         piece = row_raw.at[q * 2 + 1 - core]
         return remote(piece, piece, twin_send.at[0], twin_recv.at[q], r, twin)
 
-    for d in range(n_row - 1, 0, -1):
-
-        @pl.when(d <= r)
-        def _():
-            up_copy(d).start()
-
-    twin_copy(chip).start()
-    for d in range(1, chips):
-        far_copy(d).start()
+    @pl.loop(0, r)
+    def _(g):
+        up_copy(g).start()
+
+    @pl.when(core == 1)
+    def _():
+        twin_copy(chip).start()
+
+    @pl.loop(0, chip)
+    def _(q):
+        far_copy(q).start()
 
     padded = lists_v.shape[1]
     iota0 = lax.broadcasted_iota(I32, (slots, padded), 0)
     iota1 = lax.broadcasted_iota(I32, (slots, padded), 1)
-    listing = list_ref[0, 0]
-    local_row = listing[:, 0:1]
-    local_col = listing[:, 1:2]
-    slot = iota0[:, :1]
+    listing = jnp.concatenate(
+        [list_ref[0, 0], jnp.zeros((2, padded - slots), I32)], axis=1
+    )
+    local_row = column_of(listing[0:1], iota0 == iota1)
+    local_col = column_of(listing[1:2], iota0 == iota1)
+    live = iota0[:, :1] < count_ref[0, 0]
     diagonal = (r * (n_col * BP) + local_row) == (
         (local_col // BP) * (n_col * BP) + c * BP + local_col % BP
     )
-    weight2 = jnp.where(slot < count_ref[0, 0], jnp.where(diagonal, 1, 2), 0)
-    by_row = sorted_lists(local_row, local_col, weight2, iota0, iota1, slots)
-    by_col = sorted_lists(local_col, local_row, weight2, iota0, iota1, slots)
+    weight2 = jnp.where(live, jnp.where(diagonal, 1, 2), 0)
+    row_key = jnp.where(live, local_row, blocks)
+    col_key = jnp.where(live, local_col, blocks)
+    by_row = sorted_lists(row_key, local_col, weight2, iota0, iota1, slots)
+    by_col = sorted_lists(col_key, local_row, weight2, iota0, iota1, slots)
     lanes = lax.broadcasted_iota(I32, (slots, TILE), 1)
-    row_end, row_some = segment_ends(local_row, lanes)
-    col_end, col_some = segment_ends(local_col, lanes)
+    row_end, row_some = segment_ends(row_key, lanes)
+    col_end, col_some = segment_ends(col_key, lanes)
     for k, (order, other, again, weight) in enumerate((by_row, by_col)):
         lists_v[2 * k : 2 * k + 1] = order
         lists_v[2 * k + 1 : 2 * k + 2] = other
@@ -232,7 +246,7 @@
 
     group = 8
 
-    @pl.loop(0, chunks)
+    @pl.loop(0, parts)
     def _(k):
         tile_copy(k).wait()
 
@@ -247,16 +261,25 @@
     lists_copy.wait()
     marks_copy.wait()
 
-    for g in range(1, n_row):
-
-        @pl.when(g > r)
-        def _():
-            up_arrival(g).wait_recv()
+    @pl.loop(r + 1, n_row)
+    def _(g):
+        up_arrival(g).wait_recv()
 
     @pl.loop(0, n_row)
     def _(g):
         for b in range(BP):
             put_operand(col_x, g * BP + b, col_raw[g, b])
+
+    @pl.when(core == 0)
+    def _():
+        twin_arrival(chip).wait_recv()
+        twin_copy(chip).start()
+
+    @pl.loop(chip + 1, chips)
+    def _(q):
+        far_arrival(q).wait_recv()
+        far_copy(q).start()
+        twin_copy(q).start()
 
     def products(which, operand, forward, between):
         order_at, other_at = 2 * which, 2 * which + 1
@@ -278,16 +301,16 @@
                 running[k] = total
             return total
 
-        lax.fori_loop(0, slots // unroll, body, jnp.zeros((width, TILE), F32))
+        lax.fori_loop(0, steps, body, jnp.zeros((width, TILE), F32))
 
     def hand_over(s):
-        @pl.when((s >= 1) & (s < chips))
+        @pl.when(s == steps // 2)
         def _():
-            q = chip_at(s)
-            far_arrival(q).wait_recv()
-            twin_copy(q).start()
-
-    assert slots // unroll >= chips
+            @pl.loop(0, chip)
+            def _(q):
+                far_arrival(q).wait_recv()
+                twin_copy(q).start()
+
     products(0, col_x, True, hand_over)
 
     @pl.loop(0, n_col)
@@ -301,40 +324,45 @@
     )
     fold.start()
 
-    for q in range(chips):
-        twin_arrival(q).wait_recv()
+    @pl.when(core == 1)
+    def _():
+        twin_arrival(chip).wait_recv()
+
+    for d in range(1, chips):
+        twin_arrival((chip + d) % chips).wait_recv()
 
     @pl.loop(0, n_col)
     def _(p):
         for b in range(BP):
             put_operand(row_x, p * BP + b, row_raw[p, b])
 
-    def back_copy(d):
-        q = chip_at(d)
+    def back_copy(q):
         return remote(
             row_part.at[core, q],
             from_row.at[chip],
-            back_send.at[d],
+            back_send.at[q],
             back_recv.at[chip],
             r,
             q * 2 + core,
         )
 
-    def back_arrival(d):
-        q = chip_at(d)
+    def back_arrival(q):
         return remote(
             from_row.at[q], from_row.at[q], back_send.at[0], back_recv.at[q], r, twin
         )
 
     def fold_in(s):
-        @pl.when(s == 2)
+        @pl.when(s == jnp.minimum(steps - 1, 5))
         def _():
             fold.wait_recv()
-            for d in range(chips):
-                q = chip_at(d)
+
+            @pl.loop(1, chips)
+            def _(d):
+                q = (chip + d) % chips
                 row_part[core, q] = row_part[core, q] + from_twin[q]
-                if d > 0:
-                    back_copy(d).start()
+                back_copy(q).start()
+
+            row_part[core, chip] = row_part[core, chip] + from_twin[chip]
 
     products(1, row_x, False, fold_in)
 
@@ -344,10 +372,9 @@
             k = lists_s[5, g * BP + b]
             col_part[g, b] = running[k] * marks_s[5, g * BP + b]
 
-    def down_copy(d):
-        g = (r + d) % n_row
+    def down_copy(g):
         return remote(
-            col_part.at[g], from_col.at[r], down_send.at[d], down_recv.at[r], g, c
+            col_part.at[g], from_col.at[r], down_send.at[g], down_recv.at[r], g, c
         )
 
     def down_arrival(g):
@@ -355,44 +382,48 @@
             from_col.at[g], from_col.at[g], down_send.at[0], down_recv.at[g], r, twin
         )
 
-    for d in range(n_row - 1, 0, -1):
-
-        @pl.when(r + d < n_row)
-        def _():
-            down_copy(d).start()
+    @pl.loop(r + 1, n_row)
+    def _(g):
+        down_copy(g).start()
 
     row_part[core, chip] = row_part[core, chip] + col_part[r]
     for d in range(1, chips):
-        back_arrival(d).wait_recv()
-        row_part[core, chip] = row_part[core, chip] + from_row[chip_at(d)]
-    for g in range(n_row - 1):
-
-        @pl.when(g < r)
-        def _():
-            down_arrival(g).wait_recv()
-            row_part[core, chip] = row_part[core, chip] + from_col[g]
+        q = (chip + d) % chips
+        back_arrival(q).wait_recv()
+        row_part[core, chip] = row_part[core, chip] + from_row[q]
+
+    @pl.loop(0, r)
+    def _(d):
+        g = r - 1 - d
+        down_arrival(g).wait_recv()
+        row_part[core, chip] = row_part[core, chip] + from_col[g]
 
     for b in range(BP):
-        columns = slice(b * TILE, (b + 1) * TILE)
-        out_basis[:, columns] = row_part[core, chip, b, :half]
-        out_residual[:, columns] = row_part[core, chip, b, half:]
-
-    for d in range(1, n_row):
-
-        @pl.when(d <= r)
-        def _():
-            up_copy(d).wait_send()
-
-        @pl.when(r + d < n_row)
-        def _():
-            down_copy(d).wait_send()
-
-    for d in range(1, chips):
-        far_copy(d).wait_send()
-        back_copy(d).wait_send()
+        out[:, b * TILE : (b + 1) * TILE] = row_part[core, chip, b]
+
+    @pl.loop(0, r)
+    def _(g):
+        up_copy(g).wait_send()
+
+    @pl.loop(r + 1, n_row)
+    def _(g):
+        down_copy(g).wait_send()
+
+    @pl.loop(1, chips)
+    def _(d):
+        q = (chip + d) % chips
+        far_copy(q).wait_send()
+        back_copy(q).wait_send()
+
     for q in range(chips):
         twin_copy(q).wait_send()
     fold.wait_send()
+
+
+def part_kernel(both, basis, residual):
+    half = basis.shape[0]
+    basis[...] = both[:half]
+    residual[...] = both[half:]
 
 
 def solution(mesh):
@@ -408,18 +439,19 @@
         vmem = pl.BlockSpec(memory_space=pltpu.VMEM)
         dma = pltpu.SemaphoreType.DMA
         piece = (BP, width, TILE)
+        whole = pl.BlockSpec(memory_space=pltpu.HBM)
         shape = jax.ShapeDtypeStruct(basis_block.shape, F32)
-        return pl.pallas_call(
+        both = pl.pallas_call(
             functools.partial(kernel, n_row, n_col, unroll, chunks),
-            out_shape=(shape, shape),
+            out_shape=jax.ShapeDtypeStruct((width, basis_block.shape[1]), F32),
             in_specs=[
                 vmem,
                 pl.BlockSpec(memory_space=pltpu.SMEM),
                 vmem,
                 vmem,
-                pl.BlockSpec(memory_space=pl.ANY),
+                whole,
             ],
-            out_specs=(vmem, vmem),
+            out_specs=vmem,
             scratch_shapes=[
                 pltpu.VMEM((slots, TILE, TILE), F32),
                 pltpu.VMEM((slots, 2 * TILE, TILE), BF),
@@ -456,7 +488,19 @@
                 has_side_effects=True,
                 vmem_limit_bytes=60 * 2**20,
             ),
-        )(tile_list, tile_count, basis_block, residual_block, ham_tiles)
+        )(
+            jnp.swapaxes(tile_list, 2, 3),
+            tile_count,
+            basis_block,
+            residual_block,
+            ham_tiles,
+        )
+        return pl.pallas_call(
+            part_kernel,
+            out_shape=(shape, shape),
+            in_specs=[vmem],
+            out_specs=(vmem, vmem),
+        )(both)
 
     return jax.shard_map(
         local,

time: 48 us -> 44.3 us (0.923)
  the two profiles are of different devices: /device:TPU:9 before, /device:TPU:126 now
where the time goes in v2:
time: 44.3 us; the launch traced here: 44 us
  Pallas kernels  42.7 us (96%)
  between operations  1.28 us (3%)
    pallas_call x1, Pallas kernels, local(): pl.pallas_call(functools.partial(kernel, n_row, n_col, unroll, chunks), o...  41.3 us
    pallas_call x1, Pallas kernels, local(): pl.pallas_call(part_kernel, out_shape=(shape, shape), in_specs=[vmem], ou...  1.47 us

profile of v2, /device:TPU:126, one launch (start us, length us, event | category | flops | bytes accessed | tf_op | source)
XLA Modules:
  0.0 44.0 jit_solution(14876856523254474084)
XLA Ops:
  1.3 41.3 %shard_map.68.both = f32[32,512]{1,0:T(8,128)} custom-call(s32[1,1,2,320]{3,2,1,0:T(2,128)} %bitcast.1, s32[1,1]{1,0:T(1,128)S(6)} %copy.7.count_ref, f32[16,512]{1,0:T(8,128)} %basis_ref.1, f32[16,512]{1,0:T(8,128)} %residual_ref.1, f32[1,1,320,128,128]{4,3,2,1,0:T(8,128)} %tiles_ref.1), custom_call_target="tpu_custom_call" | custom-call | tf_op jit(solution)/shard_map/pallas_call | solution.py:444
  42.6 1.5 %shard_map.69 = (f32[16,512]{1,0:T(8,128)}, f32[16,512]{1,0:T(8,128)}) custom-call(f32[32,512]{1,0:T(8,128)} %shard_map.68.both), custom_call_target="tpu_custom_call" | custom-call | tf_op jit(solution)/shard_map/pallas_call | solution.py:498

commit v3 on v2

--- a/solution.py
+++ b/solution.py
@@ -10,8 +10,6 @@
 MESH = pl.DeviceIdType.MESH
 TILE = 128
 BP = 4
-NT = (((1,), (1,)), ((), ()))
-NN = (((1,), (0,)), ((), ()))
 BF = jnp.bfloat16
 F32 = jnp.float32
 I32 = jnp.int32
@@ -77,6 +75,7 @@
     out,
     raw,
     halves,
+    turned,
     running,
     row_raw,
     col_raw,
@@ -93,13 +92,20 @@
     marks_s,
     tile_sem,
     list_sem,
-    far_send,
-    far_recv,
+    near_sem,
+    in_sem,
+    side_send,
+    side_recv,
+    ring_send,
+    ring_recv,
+    pass_send,
+    pass_recv,
     twin_send,
     twin_recv,
     up_send,
     up_recv,
-    fold_sem,
+    fold_send,
+    fold_recv,
     back_send,
     back_recv,
     down_send,
@@ -110,23 +116,25 @@
     half = width // 2
     chips = n_col // 2
     per = slots // chunks
+    ring = raw.shape[0]
     blocks = n_col * BP
     r = lax.axis_index("row")
     c = lax.axis_index("col")
     core = c % 2
     chip = c // 2
     twin = chip * 2 + 1 - core
+    zs, z, xl = chips // 2, chip // 2, chip % 2
+    side = (z * 2 + 1 - xl) * 2 + core
 
     upper = (n_row - 1 - r) * (BP * blocks) + BP * BP * c + BP * (BP + 1) // 2
     most = (n_row - 1) * (BP * blocks) + BP * BP * (n_col - 1) + BP * (BP + 1) // 2
     bound = jnp.minimum(slots * upper // most + 1, slots)
     steps = (bound + unroll - 1) // unroll
-    parts = (bound + per - 1) // per
+    parts = (steps * unroll + per - 1) // per
 
     def tile_copy(k):
-        part = pl.ds(k * per, per)
         return pltpu.make_async_copy(
-            tiles_ref.at[0, 0, part], raw.at[part], tile_sem.at[k]
+            tiles_ref.at[0, 0, pl.ds(k * per, per)], raw.at[k % ring], tile_sem.at[k % ring]
         )
 
     def remote(src, dst, send, recv, row, col):
@@ -139,7 +147,7 @@
             device_id_type=MESH,
         )
 
-    @pl.loop(0, parts)
+    @pl.loop(0, jnp.minimum(parts, ring))
     def _(k):
         tile_copy(k).start()
 
@@ -175,20 +183,51 @@
     def _():
         pl.semaphore_wait(barrier, r + chip + core)
 
+    @pl.loop(0, z * 2)
+    def _(q):
+        pl.semaphore_signal(
+            in_sem, inc=1, device_id=(r, q * 2 + core), device_id_type=MESH
+        )
+
+    @pl.when(xl == 1)
+    def _():
+        pl.semaphore_signal(near_sem, inc=1, device_id=(r, side), device_id_type=MESH)
+
+    @pl.when(core == 1)
+    def _():
+        pl.semaphore_signal(near_sem, inc=1, device_id=(r, twin), device_id_type=MESH)
+
     def up_copy(g):
         return remote(col_raw.at[r], col_raw.at[r], up_send.at[g], up_recv.at[r], g, c)
 
     def up_arrival(g):
         return remote(col_raw.at[g], col_raw.at[g], up_send.at[0], up_recv.at[g], r, twin)
 
-    def far_copy(q):
+    def side_copy():
+        return remote(row_raw.at[c], row_raw.at[c], side_send.at[0], side_recv.at[0], r, side)
+
+    def side_arrival():
         return remote(
-            row_raw.at[c], row_raw.at[c], far_send.at[q], far_recv.at[chip], r, q * 2 + core
-        )
-
-    def far_arrival(q):
-        piece = row_raw.at[q * 2 + core]
-        return remote(piece, piece, far_send.at[0], far_recv.at[q], r, twin)
+            row_raw.at[side], row_raw.at[side], side_send.at[0], side_recv.at[0], r, side
+        )
+
+    def ring_copy(v):
+        to = (v * 2 + xl) * 2 + core
+        return remote(row_raw.at[c], row_raw.at[c], ring_send.at[v], ring_recv.at[z], r, to)
+
+    def ring_arrival(v):
+        piece = row_raw.at[(v * 2 + xl) * 2 + core]
+        return remote(piece, piece, ring_send.at[0], ring_recv.at[v], r, side)
+
+    def pass_copy(v):
+        to = (v * 2 + xl) * 2 + core
+        return remote(
+            row_raw.at[side], row_raw.at[side], pass_send.at[v], pass_recv.at[z], r, to
+        )
+
+    def pass_arrival(v):
+        piece = row_raw.at[(v * 2 + 1 - xl) * 2 + core]
+        return remote(piece, piece, pass_send.at[0], pass_recv.at[v], r, side)
 
     def twin_copy(q):
         piece = row_raw.at[q * 2 + core]
@@ -206,9 +245,13 @@
     def _():
         twin_copy(chip).start()
 
-    @pl.loop(0, chip)
-    def _(q):
-        far_copy(q).start()
+    @pl.when(xl == 1)
+    def _():
+        side_copy().start()
+
+    @pl.loop(0, z)
+    def _(v):
+        ring_copy(v).start()
 
     padded = lists_v.shape[1]
     iota0 = lax.broadcasted_iota(I32, (slots, padded), 0)
@@ -244,7 +287,7 @@
     lists_copy.start()
     marks_copy.start()
 
-    group = 8
+    group = min(per, 20)
 
     @pl.loop(0, parts)
     def _(k):
@@ -253,10 +296,69 @@
         @pl.loop(0, per // group)
         def _(s):
             for u in range(group):
-                t = k * per + s * group + u
-                hi, lo = split2(raw[t])
+                at = s * group + u
+                hi, lo = split2(raw[k % ring, at])
+                t = k * per + at
                 halves[t, :TILE] = hi
                 halves[t, TILE:] = lo
+                turned[t, :TILE] = hi.T
+                turned[t, TILE:] = lo.T
+
+        @pl.when(k + ring < parts)
+        def _():
+            tile_copy(k + ring).start()
+
+        @pl.when(k == jnp.minimum(parts, 2) - 1)
+        def _():
+            @pl.when(1 - xl + 1 - core > 0)
+            def _():
+                pl.semaphore_wait(near_sem, 1 - xl + 1 - core)
+
+            @pl.when(xl == 0)
+            def _():
+                side_copy().start()
+
+            @pl.when(core == 0)
+            def _():
+                twin_copy(chip).start()
+
+        @pl.when(k == jnp.minimum(parts, 6) - 1)
+        def _():
+            @pl.when(zs - 1 - z > 0)
+            def _():
+                pl.semaphore_wait(in_sem, 2 * (zs - 1 - z))
+
+            @pl.loop(z + 1, zs)
+            def _(v):
+                ring_copy(v).start()
+
+            side_arrival().wait_recv()
+
+            @pl.loop(1, zs)
+            def _(d):
+                pass_copy((z + d) % zs).start()
+
+            twin_copy(z * 2 + 1 - xl).start()
+
+    busy = r < 2
+
+    def hand_ring():
+        @pl.loop(1, zs)
+        def _(d):
+            v = (z + d) % zs
+            ring_arrival(v).wait_recv()
+            twin_copy(v * 2 + xl).start()
+
+    def hand_pass():
+        @pl.loop(1, zs)
+        def _(d):
+            v = (z + d) % zs
+            pass_arrival(v).wait_recv()
+            twin_copy(v * 2 + 1 - xl).start()
+
+    @pl.when(busy)
+    def _():
+        hand_ring()
 
     lists_copy.wait()
     marks_copy.wait()
@@ -270,18 +372,7 @@
         for b in range(BP):
             put_operand(col_x, g * BP + b, col_raw[g, b])
 
-    @pl.when(core == 0)
-    def _():
-        twin_arrival(chip).wait_recv()
-        twin_copy(chip).start()
-
-    @pl.loop(chip + 1, chips)
-    def _(q):
-        far_arrival(q).wait_recv()
-        far_copy(q).start()
-        twin_copy(q).start()
-
-    def products(which, operand, forward, between):
+    def products(which, operand, tiles, between):
         order_at, other_at = 2 * which, 2 * which + 1
 
         def body(s, total):
@@ -290,12 +381,7 @@
                 k = s * unroll + u
                 t = lists_s[order_at, k]
                 o = lists_s[other_at, k]
-                tile = halves[t]
-                if forward:
-                    tile = jnp.concatenate([tile[:TILE], tile[TILE:]], axis=1)
-                term = lax.dot_general(
-                    operand[o], tile, NT if forward else NN, preferred_element_type=F32
-                )
+                term = jnp.dot(operand[o], tiles[t], preferred_element_type=F32)
                 term = term[:width] + term[width:]
                 total = total * marks_s[2 * which, k] + term * marks_s[2 * which + 1, k]
                 running[k] = total
@@ -304,14 +390,11 @@
         lax.fori_loop(0, steps, body, jnp.zeros((width, TILE), F32))
 
     def hand_over(s):
-        @pl.when(s == steps // 2)
+        @pl.when(busy & (s == steps // 2))
         def _():
-            @pl.loop(0, chip)
-            def _(q):
-                far_arrival(q).wait_recv()
-                twin_copy(q).start()
-
-    products(0, col_x, True, hand_over)
+            hand_pass()
+
+    products(0, col_x, turned, hand_over)
 
     @pl.loop(0, n_col)
     def _(p):
@@ -319,22 +402,13 @@
             k = lists_s[4, p * BP + b]
             row_part[p % 2, p // 2, b] = running[k] * marks_s[4, p * BP + b]
 
-    fold = remote(
-        row_part.at[1 - core], from_twin, fold_sem.at[0], fold_sem.at[1], r, twin
-    )
-    fold.start()
-
-    @pl.when(core == 1)
-    def _():
-        twin_arrival(chip).wait_recv()
-
-    for d in range(1, chips):
-        twin_arrival((chip + d) % chips).wait_recv()
-
-    @pl.loop(0, n_col)
-    def _(p):
-        for b in range(BP):
-            put_operand(row_x, p * BP + b, row_raw[p, b])
+    def fold_copy(q):
+        return remote(
+            row_part.at[1 - core, q], from_twin.at[q], fold_send.at[q], fold_recv.at[q], r, twin
+        )
+
+    for d in range(1, chips + 1):
+        fold_copy((chip + d) % chips).start()
 
     def back_copy(q):
         return remote(
@@ -351,20 +425,38 @@
             from_row.at[q], from_row.at[q], back_send.at[0], back_recv.at[q], r, twin
         )
 
+    def add_twin():
+        @pl.loop(1, chips)
+        def _(d):
+            q = (chip + d) % chips
+            fold_copy(q).wait_recv()
+            row_part[core, q] = row_part[core, q] + from_twin[q]
+            back_copy(q).start()
+
+        fold_copy(chip).wait_recv()
+        row_part[core, chip] = row_part[core, chip] + from_twin[chip]
+
+    @pl.when(jnp.logical_not(busy))
+    def _():
+        add_twin()
+        hand_ring()
+        hand_pass()
+
+
+    for q in range(chips):
+        twin_arrival(q).wait_recv()
+
+    @pl.loop(0, n_col)
+    def _(p):
+        for b in range(BP):
+            put_operand(row_x, p * BP + b, row_raw[p, b])
+
     def fold_in(s):
-        @pl.when(s == jnp.minimum(steps - 1, 5))
+        @pl.when(busy & (s == jnp.minimum(steps - 1, 1)))
         def _():
-            fold.wait_recv()
-
-            @pl.loop(1, chips)
-            def _(d):
-                q = (chip + d) % chips
-                row_part[core, q] = row_part[core, q] + from_twin[q]
-                back_copy(q).start()
-
-            row_part[core, chip] = row_part[core, chip] + from_twin[chip]
-
-    products(1, row_x, False, fold_in)
+            add_twin()
+
+    products(1, row_x, halves, fold_in)
 
     @pl.loop(0, n_row)
     def _(g):
@@ -412,12 +504,18 @@
     @pl.loop(1, chips)
     def _(d):
         q = (chip + d) % chips
-        far_copy(q).wait_send()
         back_copy(q).wait_send()
+
+    side_copy().wait_send()
+
+    @pl.loop(1, zs)
+    def _(d):
+        ring_copy((z + d) % zs).wait_send()
+        pass_copy((z + d) % zs).wait_send()
 
     for q in range(chips):
         twin_copy(q).wait_send()
-    fold.wait_send()
+        fold_copy(q).wait_send()
 
 
 def part_kernel(both, basis, residual):
@@ -434,8 +532,9 @@
         slots = ham_tiles.shape[2]
         width = 2 * basis_block.shape[0]
         padded = -(-slots // TILE) * TILE
-        unroll = 20 if slots % 20 == 0 else 4
-        chunks = 8
+        unroll = 32 if slots % 32 == 0 else 20
+        chunks = 16
+        ring = 4
         vmem = pl.BlockSpec(memory_space=pltpu.VMEM)
         dma = pltpu.SemaphoreType.DMA
         piece = (BP, width, TILE)
@@ -453,7 +552,8 @@
             ],
             out_specs=vmem,
             scratch_shapes=[
-                pltpu.VMEM((slots, TILE, TILE), F32),
+                pltpu.VMEM((ring, slots // chunks, TILE, TILE), F32),
+                pltpu.VMEM((slots, 2 * TILE, TILE), BF),
                 pltpu.VMEM((slots, 2 * TILE, TILE), BF),
                 pltpu.VMEM((slots, width, TILE), F32),
                 pltpu.VMEM((n_col,) + piece, F32),
@@ -469,15 +569,22 @@
                 pltpu.SMEM((8, padded), I32),
                 pltpu.VMEM((8, padded), F32),
                 pltpu.SMEM((8, padded), F32),
-                dma((chunks,)),
+                dma((ring,)),
                 dma((2,)),
-                dma((chips,)),
-                dma((chips,)),
+                pltpu.SemaphoreType.REGULAR,
+                pltpu.SemaphoreType.REGULAR,
+                dma((1,)),
+                dma((1,)),
+                dma((chips // 2,)),
+                dma((chips // 2,)),
+                dma((chips // 2,)),
+                dma((chips // 2,)),
                 dma((chips,)),
                 dma((chips,)),
                 dma((n_row,)),
                 dma((n_row,)),
-                dma((2,)),
+                dma((chips,)),
+                dma((chips,)),
                 dma((chips,)),
                 dma((chips,)),
                 dma((n_row,)),

time: 44.3 us -> 37.6 us (0.85)
  the two profiles are of different devices: /device:TPU:126 before, /device:TPU:62 now
where the time goes in v3:
time: 37.6 us; the launch traced here: 37.3 us
  Pallas kernels  36 us (96%)
  between operations  1.28 us (3%)
    pallas_call x1, Pallas kernels, local(): pl.pallas_call(functools.partial(kernel, n_row, n_col, unroll, chunks), o...  34.5 us
    pallas_call x1, Pallas kernels, local(): pl.pallas_call(part_kernel, out_shape=(shape, shape), in_specs=[vmem], ou...  1.47 us

profile of v3, /device:TPU:62, one launch (start us, length us, event | category | flops | bytes accessed | tf_op | source)
XLA Modules:
  0.0 37.3 jit_solution(10810574059550002973)
XLA Ops:
  1.3 34.5 %shard_map.68.both = f32[32,512]{1,0:T(8,128)} custom-call(s32[1,1,2,320]{3,2,1,0:T(2,128)} %bitcast.1, s32[1,1]{1,0:T(1,128)S(6)} %copy.7.count_ref, f32[16,512]{1,0:T(8,128)} %basis_ref.1, f32[16,512]{1,0:T(8,128)} %residual_ref.1, f32[1,1,320,128,128]{4,3,2,1,0:T(8,128)} %tiles_ref.1), custom_call_target="tpu_custom_call" | custom-call | tf_op jit(solution)/shard_map/pallas_call | solution.py:543
  35.8 1.5 %shard_map.69 = (f32[16,512]{1,0:T(8,128)}, f32[16,512]{1,0:T(8,128)}) custom-call(f32[32,512]{1,0:T(8,128)} %shard_map.68.both), custom_call_target="tpu_custom_call" | custom-call | tf_op jit(solution)/shard_map/pallas_call | solution.py:605

commit v4 on v3

--- a/solution.py
+++ b/solution.py
@@ -474,9 +474,9 @@
             from_col.at[g], from_col.at[g], down_send.at[0], down_recv.at[g], r, twin
         )
 
-    @pl.loop(r + 1, n_row)
-    def _(g):
-        down_copy(g).start()
+    @pl.loop(0, n_row - 1 - r)
+    def _(d):
+        down_copy(n_row - 1 - d).start()
 
     row_part[core, chip] = row_part[core, chip] + col_part[r]
     for d in range(1, chips):
@@ -532,7 +532,7 @@
         slots = ham_tiles.shape[2]
         width = 2 * basis_block.shape[0]
         padded = -(-slots // TILE) * TILE
-        unroll = 32 if slots % 32 == 0 else 20
+        unroll = 80
         chunks = 16
         ring = 4
         vmem = pl.BlockSpec(memory_space=pltpu.VMEM)

time: 37.6 us -> 36.8 us (0.979)
  the two profiles are of different devices: /device:TPU:62 before, /device:TPU:6 now
where the time goes in v4:
time: 36.8 us; the launch traced here: 36.5 us
  Pallas kernels  35.2 us (96%)
  between operations  1.28 us (3%)
    pallas_call x1, Pallas kernels, local(): pl.pallas_call(functools.partial(kernel, n_row, n_col, unroll, chunks), o...  33.7 us
    pallas_call x1, Pallas kernels, local(): pl.pallas_call(part_kernel, out_shape=(shape, shape), in_specs=[vmem], ou...  1.47 us

profile of v4, /device:TPU:6, one launch (start us, length us, event | category | flops | bytes accessed | tf_op | source)
XLA Modules:
  0.0 36.5 jit_solution(13871788719656810156)
XLA Ops:
  1.3 33.7 %shard_map.68.both = f32[32,512]{1,0:T(8,128)} custom-call(s32[1,1,2,320]{3,2,1,0:T(2,128)} %bitcast.1, s32[1,1]{1,0:T(1,128)S(6)} %copy.7.count_ref, f32[16,512]{1,0:T(8,128)} %basis_ref.1, f32[16,512]{1,0:T(8,128)} %residual_ref.1, f32[1,1,320,128,128]{4,3,2,1,0:T(8,128)} %tiles_ref.1), custom_call_target="tpu_custom_call" | custom-call | tf_op jit(solution)/shard_map/pallas_call | solution.py:543
  35.0 1.5 %shard_map.69 = (f32[16,512]{1,0:T(8,128)}, f32[16,512]{1,0:T(8,128)}) custom-call(f32[32,512]{1,0:T(8,128)} %shard_map.68.both), custom_call_target="tpu_custom_call" | custom-call | tf_op jit(solution)/shard_map/pallas_call | solution.py:605

commit v5 on v4

--- a/solution.py
+++ b/solution.py
@@ -90,6 +90,8 @@
     lists_s,
     marks_v,
     marks_s,
+    list_v,
+    own_sem,
     tile_sem,
     list_sem,
     near_sem,
@@ -147,16 +149,25 @@
             device_id_type=MESH,
         )
 
+    own = []
+    for b in range(BP):
+        columns = pl.ds(b * TILE, TILE)
+        for k, ref in enumerate((basis_ref, residual_ref)):
+            own.append(
+                pltpu.make_async_copy(
+                    ref.at[:, columns],
+                    row_raw.at[c, b, pl.ds(k * half, half)],
+                    own_sem.at[2 * b + k],
+                )
+            )
+    own.append(pltpu.make_async_copy(list_ref, list_v, own_sem.at[2 * BP]))
+    for copy in own:
+        copy.start()
+
     @pl.loop(0, jnp.minimum(parts, ring))
     def _(k):
         tile_copy(k).start()
 
-    for b in range(BP):
-        columns = slice(b * TILE, (b + 1) * TILE)
-        row_raw[c, b, :half] = basis_ref[:, columns]
-        row_raw[c, b, half:] = residual_ref[:, columns]
-        col_raw[r, b, :half] = basis_ref[:, columns]
-        col_raw[r, b, half:] = residual_ref[:, columns]
     for g in range(n_row):
 
         @pl.when(g < r)
@@ -183,6 +194,9 @@
     def _():
         pl.semaphore_wait(barrier, r + chip + core)
 
+    for copy in own[:-1]:
+        copy.wait()
+
     @pl.loop(0, z * 2)
     def _(q):
         pl.semaphore_signal(
@@ -198,7 +212,7 @@
         pl.semaphore_signal(near_sem, inc=1, device_id=(r, twin), device_id_type=MESH)
 
     def up_copy(g):
-        return remote(col_raw.at[r], col_raw.at[r], up_send.at[g], up_recv.at[r], g, c)
+        return remote(row_raw.at[c], col_raw.at[r], up_send.at[g], up_recv.at[r], g, c)
 
     def up_arrival(g):
         return remote(col_raw.at[g], col_raw.at[g], up_send.at[0], up_recv.at[g], r, twin)
@@ -253,11 +267,14 @@
     def _(v):
         ring_copy(v).start()
 
+    col_raw[r] = row_raw[c]
+    own[-1].wait()
+
     padded = lists_v.shape[1]
     iota0 = lax.broadcasted_iota(I32, (slots, padded), 0)
     iota1 = lax.broadcasted_iota(I32, (slots, padded), 1)
     listing = jnp.concatenate(
-        [list_ref[0, 0], jnp.zeros((2, padded - slots), I32)], axis=1
+        [list_v[0, 0], jnp.zeros((2, padded - slots), I32)], axis=1
     )
     local_row = column_of(listing[0:1], iota0 == iota1)
     local_col = column_of(listing[1:2], iota0 == iota1)
@@ -340,7 +357,7 @@
 
             twin_copy(z * 2 + 1 - xl).start()
 
-    busy = r < 2
+    busy = r < 3
 
     def hand_ring():
         @pl.loop(1, zs)
@@ -532,7 +549,7 @@
         slots = ham_tiles.shape[2]
         width = 2 * basis_block.shape[0]
         padded = -(-slots // TILE) * TILE
-        unroll = 80
+        unroll = 80 if slots % 80 == 0 else 16
         chunks = 16
         ring = 4
         vmem = pl.BlockSpec(memory_space=pltpu.VMEM)
@@ -544,10 +561,10 @@
             functools.partial(kernel, n_row, n_col, unroll, chunks),
             out_shape=jax.ShapeDtypeStruct((width, basis_block.shape[1]), F32),
             in_specs=[
-                vmem,
+                whole,
                 pl.BlockSpec(memory_space=pltpu.SMEM),
-                vmem,
-                vmem,
+                whole,
+                whole,
                 whole,
             ],
             out_specs=vmem,
@@ -569,6 +586,8 @@
                 pltpu.SMEM((8, padded), I32),
                 pltpu.VMEM((8, padded), F32),
                 pltpu.SMEM((8, padded), F32),
+                pltpu.VMEM((1, 1, 2, slots), I32),
+                dma((2 * BP + 1,)),
                 dma((ring,)),
                 dma((2,)),
                 pltpu.SemaphoreType.REGULAR,

time: 36.8 us -> 36.2 us (0.984)
  Pallas kernels: 35.2 us -> 34.7 us
    pallas_call x1, Pallas kernels: 33.7 us -> 33.3 us  [local(): pl.pallas_call(functools.partial(kernel, n_row, n_col, unroll, chunks), o...]
where the time goes in v5:
time: 36.2 us; the launch traced here: 36 us
  Pallas kernels  34.7 us (96%)
  between operations  1.28 us (4%)
    pallas_call x1, Pallas kernels, local(): pl.pallas_call(functools.partial(kernel, n_row, n_col, unroll, chunks), o...  33.3 us
    pallas_call x1, Pallas kernels, local(): pl.pallas_call(part_kernel, out_shape=(shape, shape), in_specs=[vmem], ou...  1.47 us

profile of v5, /device:TPU:6, one launch (start us, length us, event | category | flops | bytes accessed | tf_op | source)
XLA Modules:
  0.0 36.0 jit_solution(14422417693978363675)
XLA Ops:
  1.3 33.3 %shard_map.68.both = f32[32,512]{1,0:T(8,128)} custom-call(s32[1,1,2,320]{3,2,1,0:T(2,128)} %bitcast.1, s32[1,1]{1,0:T(1,128)S(6)} %copy.7.count_ref, f32[16,512]{1,0:T(8,128)} %basis_ref.1, f32[16,512]{1,0:T(8,128)} %residual_ref.1, f32[1,1,320,128,128]{4,3,2,1,0:T(8,128)} %tiles_ref.1), custom_call_target="tpu_custom_call" | custom-call | tf_op jit(solution)/shard_map/pallas_call | solution.py:560
  34.5 1.5 %shard_map.69 = (f32[16,512]{1,0:T(8,128)}, f32[16,512]{1,0:T(8,128)}) custom-call(f32[32,512]{1,0:T(8,128)} %shard_map.68.both), custom_call_target="tpu_custom_call" | custom-call | tf_op jit(solution)/shard_map/pallas_call | solution.py:624

commit v6 on v5

--- a/solution.py
+++ b/solution.py
@@ -91,6 +91,8 @@
     marks_v,
     marks_s,
     list_v,
+    out_v,
+    out_sem,
     own_sem,
     tile_sem,
     list_sem,
@@ -508,7 +510,9 @@
         row_part[core, chip] = row_part[core, chip] + from_col[g]
 
     for b in range(BP):
-        out[:, b * TILE : (b + 1) * TILE] = row_part[core, chip, b]
+        out_v[:, b * TILE : (b + 1) * TILE] = row_part[core, chip, b]
+    result = pltpu.make_async_copy(out_v, out, out_sem.at[0])
+    result.start()
 
     @pl.loop(0, r)
     def _(g):
@@ -533,6 +537,7 @@
     for q in range(chips):
         twin_copy(q).wait_send()
         fold_copy(q).wait_send()
+    result.wait()
 
 
 def part_kernel(both, basis, residual):
@@ -567,7 +572,7 @@
                 whole,
                 whole,
             ],
-            out_specs=vmem,
+            out_specs=whole,
             scratch_shapes=[
                 pltpu.VMEM((ring, slots // chunks, TILE, TILE), F32),
                 pltpu.VMEM((slots, 2 * TILE, TILE), BF),
@@ -587,6 +592,8 @@
                 pltpu.VMEM((8, padded), F32),
                 pltpu.SMEM((8, padded), F32),
                 pltpu.VMEM((1, 1, 2, slots), I32),
+                pltpu.VMEM((width, basis_block.shape[1]), F32),
+                dma((1,)),
                 dma((2 * BP + 1,)),
                 dma((ring,)),
                 dma((2,)),

time: 36.2 us -> 36 us (level)
  no operation moved by 1% of the time
where the time goes in v6:
time: 36 us; the launch traced here: 35.8 us
  Pallas kernels  34.5 us (96%)
  between operations  1.28 us (4%)
    pallas_call x1, Pallas kernels, local(): pl.pallas_call(functools.partial(kernel, n_row, n_col, unroll, chunks), o...  33 us
    pallas_call x1, Pallas kernels, local(): pl.pallas_call(part_kernel, out_shape=(shape, shape), in_specs=[vmem], ou...  1.47 us

profile of v6, /device:TPU:6, one launch (start us, length us, event | category | flops | bytes accessed | tf_op | source)
XLA Modules:
  0.0 35.8 jit_solution(2492936157322834956)
XLA Ops:
  1.3 33.0 %shard_map.68.both = f32[32,512]{1,0:T(8,128)} custom-call(s32[1,1,2,320]{3,2,1,0:T(2,128)} %bitcast.1, s32[1,1]{1,0:T(1,128)S(6)} %copy.7.count_ref, f32[16,512]{1,0:T(8,128)} %basis_ref.1, f32[16,512]{1,0:T(8,128)} %residual_ref.1, f32[1,1,320,128,128]{4,3,2,1,0:T(8,128)} %tiles_ref.1), custom_call_target="tpu_custom_call" | custom-call | tf_op jit(solution)/shard_map/pallas_call | solution.py:565
  34.3 1.5 %shard_map.69 = (f32[16,512]{1,0:T(8,128)}, f32[16,512]{1,0:T(8,128)}) custom-call(f32[32,512]{1,0:T(8,128)} %shard_map.68.both), custom_call_target="tpu_custom_call" | custom-call | tf_op jit(solution)/shard_map/pallas_call | solution.py:631
